TPU v7x, 32 devices: a whole 2x2x4 slice. The times are simulated.
32 devices in a mesh: dp: 8 (over z, y), mp: 4 (over x, core).
Axes of the slice: x: 2, y: 2, z: 4, core: 2. Of those that a mesh axis runs over, the one named last changes fastest.
Arguments:
- inputs: bfloat16 [8192, 1024], P(('dp', 'mp')), may hold values from -6 to 6
- teacher: bfloat16 [8192, 1024], P(('dp', 'mp')), may hold values from -6 to 6
- segments: int32 [8, 1024], P('dp'), may hold values from 0 to 7, never falling along the last dimension, each value on 1 to 768 neighbouring positions
- valid_mask: int32 [8192], P(('dp', 'mp')), may hold values from 0 to 1, as said below
- qkv_copy: bfloat16 [1024, 3, 1024], P(None, None, 'mp'), may hold values from -0.1875 to 0.1875
- out_copy: bfloat16 [1024, 1024], P('mp'), may hold values from -0.5 to 0.5
- up_copy: bfloat16 [1024, 4096], P(None, 'mp'), may hold values from -0.1875 to 0.1875
- down_copy: bfloat16 [4096, 1024], P('mp'), may hold values from -0.09375 to 0.09375
- vector_copy: bfloat16 [12, 1024], replicated
- qkv_state: float32 [3, 1024, 3, 1024], P(None, 'dp', None, 'mp'), as said below
- out_state: float32 [3, 1024, 1024], P(None, 'mp', 'dp'), as said below
- up_state: float32 [3, 1024, 4096], P(None, 'dp', 'mp'), as said below
- down_state: float32 [3, 4096, 1024], P(None, 'mp', 'dp'), as said below
- vector_state: float32 [3, 12, 1024], replicated, as said below
Outputs:
- block_out: bfloat16 [8192, 1024], P(('dp', 'mp'))
- input_grad: float32 [8192, 1024], P(('dp', 'mp'))
- qkv_grad: float32 [1024, 3, 1024], P('dp', None, 'mp')
- out_grad: float32 [1024, 1024], P('mp', 'dp')
- up_grad: float32 [1024, 4096], P('dp', 'mp')
- down_grad: float32 [4096, 1024], P('mp', 'dp')
- vector_grad: float32 [12, 1024], replicated
- qkv_state_new: float32 [3, 1024, 3, 1024], P(None, 'dp', None, 'mp')
- out_state_new: float32 [3, 1024, 1024], P(None, 'mp', 'dp')
- up_state_new: float32 [3, 1024, 4096], P(None, 'dp', 'mp')
- down_state_new: float32 [3, 4096, 1024], P(None, 'mp', 'dp')
- vector_state_new: float32 [3, 12, 1024], replicated
- qkv_copy_new: bfloat16 [1024, 3, 1024], P(None, None, 'mp')
- out_copy_new: bfloat16 [1024, 1024], P('mp')
- up_copy_new: bfloat16 [1024, 4096], P(None, 'mp')
- down_copy_new: bfloat16 [4096, 1024], P('mp')
- vector_copy_new: bfloat16 [12, 1024], replicated
Inputs may be any that keep to these rules, and one draw needn't show every extreme that they name: `segments`: ids never fall along a sequence. `valid_mask`: the first token of every sequence is 1. `qkv_state`: row 2 is positive. `out_state`: row 2 is positive. `up_state`: row 2 is positive. `down_state`: row 2 is positive. `vector_state`: row 2 is positive.
All inputs are finite; a program needn't handle non-finite values.
Results may differ from a plain program's by a relative error of at most 0.007.
The roundings to bfloat16 on the way count: a program that leaves them out, or rounds other values in their place, can miss the bound.
Values may be sent and summed in bfloat16 or wider, within the bound.
A program may use at most 128 MiB of HBM per device.

v0:
```python
import functools
import math
import types

import jax
import jax.numpy as jnp
from jax import lax
from jax.experimental import pallas as pl
from jax.experimental.pallas import tpu as pltpu
from jax.sharding import PartitionSpec as P

HEADS = 16
HD = 64

norm_eps = 1e-05
beta_one = 0.9
beta_two = 0.95
adam_eps = 1e-08
learn_rate = 0.001
decay_rate = 0.1
correction_one = 1.0 - (0.9**10) ** 10
correction_two = 1.0 - (0.95**10) ** 10
log2_e = 1.4426950408889634

CHUNKS = 2
BQ = 256
TILE = 256
MESH = pl.DeviceIdType.MESH
F32 = jnp.float32
BF16 = jnp.bfloat16
NN = ((1,), (0,))
NT = ((1,), (1,))
TN = ((0,), (0,))


def mm(a, b, dims):
    return lax.dot_general(a, b, (dims, ((), ())), preferred_element_type=F32)


def gelu_both(v):
    c = 0.7978845608
    v2 = v * v
    th = jnp.tanh(c * (v + 0.044715 * v2 * v))
    half = 0.5 * (1.0 + th)
    back = half + 0.5 * v * (1.0 - th * th) * (c * (1.0 + 3.0 * 0.044715 * v2))
    return v * half, back


def norm_rows(v):
    centred = v - jnp.mean(v, -1, keepdims=True)
    inverse = lax.rsqrt(jnp.mean(centred * centred, -1, keepdims=True) + norm_eps)
    return centred * inverse, inverse


def norm_backward(grad_out, normed, inverse, gain_row):
    scaled = grad_out * gain_row
    return inverse * (
        scaled
        - jnp.mean(scaled, -1, keepdims=True)
        - normed * jnp.mean(scaled * normed, -1, keepdims=True)
    )


def adam_step(gradient, weight, first, second, decay_factor, token_total):
    mean_grad = gradient / token_total
    moment_one = beta_one * first + (1.0 - beta_one) * mean_grad
    moment_two = beta_two * second + (1.0 - beta_two) * mean_grad * mean_grad
    update = (
        moment_one / correction_one / (jnp.sqrt(moment_two / correction_two) + adam_eps)
        + decay_factor * weight
    )
    return weight - learn_rate * update, moment_one, moment_two


def block_kernel(sizes, fast, names, *refs):
    r = types.SimpleNamespace(**dict(zip(names, refs)))
    dp_size, mp_size = sizes
    dp = lax.axis_index("dp")
    m = lax.axis_index("mp")
    core = lax.rem(m, 2)
    chip = m // 2
    mc = m + 1 - 2 * core
    mx = lax.rem(m + 2, 4)
    md = mc + mx - m
    C = CHUNKS
    R, D = r.x.shape
    rc = R // C
    T = mp_size * R
    HW = r.wout.shape[0]
    FU = r.wup.shape[1]
    LOCAL_HEADS = HW // HD
    PAIR = 2 * HD
    PAIRS = HW // PAIR
    token_total = float(dp_size * T)

    dp_bits = [("dp", b) for b in range(dp_size.bit_length() - 1)]
    mp_bits = [("mp", b) for b in range(mp_size.bit_length() - 1)]
    bits = dp_bits + mp_bits

    def flip(v, b):
        w = 1 << b
        return v + w - 2 * w * lax.rem(v // w, 2)

    def bit_partner(item):
        axis, b = item
        if axis == "mp":
            return (dp, flip(m, b))
        return (flip(dp, b), m)

    to_core = (dp, mc)
    to_x = (dp, mx)

    NZ = dp_size // 2
    z = dp // 2
    y = lax.rem(dp, 2)
    to_y = (dp + 1 - 2 * y, m)

    def line(direction):
        place = z + direction * (NZ - 1 - 2 * z)
        return place, (dp + 2 - 4 * direction, m)

    def local_copy(src, dst, sem):
        cp = pltpu.make_async_copy(src, dst, sem)
        cp.start()
        return cp

    def qkv_lanes(pair, kind):
        return slice((3 * pair + kind) * PAIR, (3 * pair + kind + 1) * PAIR)

    x_in = local_copy(r.x_hbm, r.x, r.in_sem.at[0])
    t_in = local_copy(r.t_hbm, r.t, r.in_sem.at[1])
    qkv_weights = [
        local_copy(
            r.wqkv_hbm.at[kind, :, pair * PAIR : (pair + 1) * PAIR],
            r.wqkv.at[:, qkv_lanes(pair, kind)],
            r.wq_sem.at[pair, kind],
        )
        for pair in range(PAIRS)
        for kind in range(3)
    ]
    weights = [
        local_copy(src, dst, r.w_sem.at[i])
        for i, (src, dst) in enumerate(
            [(r.wout_hbm, r.wout), (r.wup_hbm, r.wup), (r.wdown_hbm, r.wdown)]
        )
    ]
    if fast:
        parts = {}
        for name, width in pieces(HW, FU):
            left, right = {
                "d": (r.g3, r.act),
                "u": (r.g2, r.gup),
                "o": (r.g4, r.mix),
                "q": (r.g1, r.st),
            }[name[0]]
            parts[name] = (len(parts), left, right, width)
        names_of = list(parts)
        state_in = {}

        def span(name):
            width = PAIR if name[0] == "q" else parts[name][3]
            return slice(int(name[1]) * width, (int(name[1]) + 1) * width)

        def piece(ref, name):
            at = span(name)
            if name[0] == "q":
                return ref.at[:, :, at]
            return ref.at[:, at] if name[0] == "u" else ref.at[at, :]

        def state_copies(name, out):
            far = getattr(r, name[0] + "_new") if out else getattr(r, "s%s_hbm" % name[0])
            at = span(name)
            if name[0] == "q":
                return [
                    (
                        far.at[:, kind, :, at],
                        r.big.at[0:3, SHARE : 2 * SHARE, kind * HW + at.start : kind * HW + at.stop],
                    )
                    for kind in range(3)
                ]
            if name[0] == "u":
                return [(far.at[:, :, at], r.big.at[0:3, 0:SHARE, at])]
            return [(far.at[:, at, :], getattr(r, "s" + name[0]).at[:, at, :])]

        def state_sem(name, k):
            p = parts[name][0]
            return r.s_sem.at[p + 2 * max(0, p - 5) + k]

        def fetch_state(matrix):
            for name in parts:
                if name[0] == matrix:
                    state_in[name] = [
                        local_copy(far, near, state_sem(name, k))
                        for k, (far, near) in enumerate(state_copies(name, False))
                    ]

        fetch_state("d")
        fetch_state("o")

    vec_in = local_copy(r.vec_state_hbm, r.vec_state, r.in_sem.at[2])
    barrier = pltpu.get_barrier_semaphore()
    for item in bits:
        pl.semaphore_signal(barrier, inc=1, device_id=bit_partner(item), device_id_type=MESH)
    greetings = len(bits)
    if fast:
        for direction in range(2):
            place, following = line(direction)

            @pl.when(place < NZ - 1)
            def _():
                pl.semaphore_signal(barrier, inc=1, device_id=following, device_id_type=MESH)

        greetings = greetings + (z > 0).astype(jnp.int32) + (z < NZ - 1).astype(jnp.int32)
    r.vec[...] = r.vec_low[...].astype(F32)
    x_in.wait()
    for j in range(C):
        rows = slice(j * rc, (j + 1) * rc)
        normed, inverse = norm_rows(r.x[rows, :].astype(F32))
        r.g1[m, rows, :] = (normed * r.vec[0:1, :] + r.vec[1:2, :]).astype(BF16)
    r.vg[...] = jnp.zeros(r.vg.shape, F32)
    r.cnt[0] = jnp.zeros((8, 128), F32) + jnp.sum(r.valid[...].astype(F32))
    pl.semaphore_wait(barrier, greetings)

    def doubling(order, values, received, send_sems, recv_sems):
        copies = []

        def send(step):
            cp = pltpu.make_async_remote_copy(
                src_ref=values.at[step], dst_ref=received.at[step],
                send_sem=send_sems.at[step], recv_sem=recv_sems.at[step],
                device_id=bit_partner(order[step]), device_id_type=MESH,
            )
            cp.start()
            copies.append(cp)

        def following():
            step = len(copies) - 1
            copies[step].wait()
            values[step + 1] = values[step] + received[step]
            if step + 1 < len(order):
                send(step + 1)

        return send, following

    count_send, count_next = doubling(bits, r.cnt, r.cnt_r, r.cnt_ss, r.cnt_rs)

    def ag_copy(site, j, kind, ref, block, device):
        part = ref.at[block, pl.ds(j * rc, rc)]
        return pltpu.make_async_remote_copy(
            src_ref=part, dst_ref=part, send_sem=r.ag_ss.at[site, j, kind],
            recv_sem=r.ag_rs.at[site, j, kind], device_id=device, device_id_type=MESH,
        )

    def ag_send(site, j, ref):
        cx = ag_copy(site, j, 0, ref, m, to_x)
        cx.start()
        cc = ag_copy(site, j, 1, ref, m, to_core)
        cc.start()
        return cx, cc

    def ag_start(site, j, ref, value):
        ref[m, pl.ds(j * rc, rc), :] = value
        return ag_send(site, j, ref)

    def ag_forward(site, j, ref):
        cf = ag_copy(site, j, 2, ref, mx, to_core)
        cf.start()
        return cf

    def rs_copy(site, j, kind, src, dst, device):
        return pltpu.make_async_remote_copy(
            src_ref=src, dst_ref=dst, send_sem=r.rs_ss.at[site - 1, j, kind],
            recv_sem=r.rs_rs.at[site - 1, j, kind], device_id=device, device_id_type=MESH,
        )

    def rs_product(j, lhs, rhs_of, slot, kept_ref):
        def tile_body(n, carry):
            lanes = pl.ds(pl.multiple_of(n * TILE, TILE), TILE)
            rhs, dims = rhs_of(lanes)
            both = mm(lhs, rhs, dims)
            low, high = both[:rc], both[rc:]
            r.rs_cs[j, slot, :, lanes] = jnp.where(core == 0, high, low).astype(BF16)
            kept_ref[j, :, lanes] = jnp.where(core == 0, low, high)
            return carry

        lax.fori_loop(0, D // TILE, tile_body, 0)

    def rs_core(site, j, slot):
        cp = rs_copy(site, j, slot, r.rs_cs.at[j, slot], r.rs_cr.at[j, slot], to_core)
        cp.start()
        return cp

    def rs_own(site, j, lhs_of, rhs_of):
        rs_product(j, lhs_of(2 * chip), rhs_of, 1, r.keep)
        return rs_core(site, j, 1)

    def rs_other(site, j, lhs_of, rhs_of, between=None):
        rs_product(j, lhs_of(2 * (1 - chip)), rhs_of, 0, r.pass_on)
        c0 = rs_core(site, j, 0)
        c1 = between() if between else None
        c0.wait()
        r.rs_xs[j] = (r.pass_on[j] + r.rs_cr[j, 0].astype(F32)).astype(BF16)
        cx = rs_copy(site, j, 2, r.rs_xs.at[j], r.rs_xr.at[j], to_x)
        cx.start()
        return cx, c1

    def rs_start(site, j, lhs_of, rhs_of):
        return rs_other(site, j, lhs_of, rhs_of, lambda: rs_own(site, j, lhs_of, rhs_of))

    def rs_finish(j, copies):
        for cp in copies:
            cp.wait()
        return r.keep[j] + r.rs_cr[j, 1].astype(F32) + r.rs_xr[j].astype(F32)

    def share_rows(ref, share):
        lanes = pl.ds(pl.multiple_of(share * SHARE, SHARE), SHARE)
        return ref[:, :, lanes].reshape(T, SHARE).T

    def right_tile(ref, lanes):
        if len(ref.shape) == 3:
            return ref[:, :, lanes].reshape(T, lanes.size)
        return ref[:, lanes]

    def tiles(width):
        return width if width < 2 * TILE else TILE

    def part_tile(name, n, step):
        _, _, right, width = parts[name]
        lanes = pl.ds(pl.multiple_of(n * step, 128), step)
        from_lanes = pl.ds(pl.multiple_of(int(name[1]) * width + n * step, 128), step)
        return lanes, right_tile(right, from_lanes)

    def part_product(name, lhs, put):
        width = parts[name][3]
        step = tiles(width)

        def tile_body(n, carry):
            lanes, rhs = part_tile(name, n, step)
            put(lanes, mm(lhs, rhs, NN))
            return carry

        lax.fori_loop(0, width // step, tile_body, 0)

    def y_copy(name, i):
        p = parts[name][0]
        return pltpu.make_async_remote_copy(
            src_ref=getattr(r, "ys" + name).at[i], dst_ref=getattr(r, "yr" + name).at[i],
            send_sem=r.y_ss.at[p, i], recv_sem=r.y_rs.at[p, i], device_id=to_y, device_id_type=MESH,
        )

    def y_start(name):
        left = parts[name][1]
        out = getattr(r, "ys" + name)

        def pair_body(i, carry):
            lhs = jnp.concatenate(
                [share_rows(left, 4 * i + 1 - y), share_rows(left, 4 * i + 3 - y)], 0
            )

            def put(lanes, both):
                out[2 * i, :, lanes] = both[:SHARE].astype(BF16)
                out[2 * i + 1, :, lanes] = both[SHARE:].astype(BF16)

            part_product(name, lhs, put)
            y_copy(name, 2 * i).start()
            y_copy(name, 2 * i + 1).start()
            return carry

        lax.fori_loop(0, NZ // 2, pair_body, 0)

    def share_sum(name, target):
        got = getattr(r, "yr" + name)
        y_copy(name, target).wait_recv()

        def put(lanes, value):
            r.acc[0:SHARE, lanes] = value + got[target, :, lanes].astype(F32)

        part_product(name, share_rows(parts[name][1], 2 * target + y), put)

    def both_shares(name, target):
        def put(lanes, value):
            r.wide[:, lanes] = value

        left = parts[name][1]
        lanes = pl.ds(pl.multiple_of(2 * target * SHARE, 2 * SHARE), 2 * SHARE)
        part_product(name, left[:, :, lanes].reshape(T, 2 * SHARE).T, put)

    def z_copy(name, direction, step, device):
        p = parts[name][0]
        return pltpu.make_async_remote_copy(
            src_ref=getattr(r, "zs" + name).at[direction],
            dst_ref=getattr(r, "zr" + name).at[direction, step],
            send_sem=r.z_ss.at[p, direction], recv_sem=r.z_rs.at[p, direction, step],
            device_id=device, device_id_type=MESH,
        )

    def chain_step(name, step):
        out = getattr(r, "zs" + name)
        got = getattr(r, "zr" + name)
        width = parts[name][3]
        total = (r.wide if name in Z_FIRST else r.acc).at[:, 0:width]

        def one(direction, carry):
            place, following = line(direction)

            @pl.when(place <= step)
            def _():
                mirrored = NZ - 1 - step + place
                target = mirrored + direction * (NZ - 1 - 2 * mirrored)
                (both_shares if name in Z_FIRST else share_sum)(name, target)
                if step > 0:

                    @pl.when(place < step)
                    def _():
                        z_copy(name, direction, step - 1, following).wait_send()

                    @pl.when(place > 0)
                    def _():
                        z_copy(name, direction, step - 1, following).wait_recv()
                        total[...] += got[direction, step - 1].astype(F32)

                out[direction] = total[...].astype(BF16)
                z_copy(name, direction, step, following).start()

            return carry

        lax.fori_loop(0, 2, one, 0)

    def chain_end(name):
        got = getattr(r, "zr" + name)
        width = parts[name][3]
        total = (r.wide if name in Z_FIRST else r.acc).at[:, 0:width]
        (both_shares if name in Z_FIRST else share_sum)(name, z)

        def one(direction, carry):
            place, _ = line(direction)

            @pl.when(place > 0)
            def _():
                z_copy(name, direction, NZ - 2, (dp, m)).wait_recv()
                total[...] += got[direction, NZ - 2].astype(F32)

            return carry

        lax.fori_loop(0, 2, one, 0)

    def y_exchange(name):
        chain_end(name)
        width = parts[name][3]
        theirs = pl.ds(pl.multiple_of((1 - y) * SHARE, SHARE), SHARE)
        getattr(r, "ys" + name)[0] = r.wide[theirs, 0:width].astype(BF16)
        y_copy(name, 0).start()

    def a_src(name, share):
        ref = getattr(r, name[0] + "_full")
        at = pl.ds(pl.multiple_of(share * SHARE, SHARE), SHARE)
        if name[0] == "q":
            return ref.at[:, at, span(name)]
        return ref.at[at, span(name)] if name[0] == "u" else ref.at[span(name), at]

    def az_copy(name, side, direction, step, share, src, device):
        p = len(parts) + Y_FIRST.index(name) if side else parts[name][0]
        return pltpu.make_async_remote_copy(
            src_ref=src, dst_ref=a_src(name, share), send_sem=r.az_ss.at[p, direction, step],
            recv_sem=r.az_rs.at[p, direction, step], device_id=device, device_id_type=MESH,
        )

    def ay_copy(name, place, src):
        p = parts[name][0]
        return pltpu.make_async_remote_copy(
            src_ref=src, dst_ref=a_src(name, 2 * place + y), send_sem=r.ay_ss.at[p, place],
            recv_sem=r.ay_rs.at[p, place], device_id=to_y, device_id_type=MESH,
        )

    local_out = []

    def finish_share(name):
        p, _, _, width = parts[name]
        matrix = name[0]
        at0 = span(name)
        if name in Z_FIRST:
            y_copy(name, 0).wait_recv()
            ours = pl.ds(pl.multiple_of(y * SHARE, SHARE), SHARE)
            r.acc[:, 0:width] = r.wide[ours, 0:width] + getattr(r, "yr" + name)[0].astype(F32)
        else:
            chain_end(name)
        for cp in state_in[name]:
            cp.wait()
        grad_out = getattr(r, "gr" + matrix)
        fresh = getattr(r, "nc" + matrix)

        def adam_block(cols, at, state, state_at):
            grad = r.acc[:, cols]
            if matrix in "do":
                grad = grad.T
            grad_out[at] = grad
            w, a, b = adam_step(
                grad,
                state[(0,) + state_at],
                state[(1,) + state_at],
                state[(2,) + state_at],
                decay_rate,
                token_total,
            )
            state[(0,) + state_at] = w
            state[(1,) + state_at] = a
            state[(2,) + state_at] = b
            fresh[at] = w.astype(BF16)

        if matrix == "q":
            for kind in range(3):
                adam_block(
                    slice(kind * PAIR, (kind + 1) * PAIR),
                    (kind, slice(None), at0),
                    r.big,
                    (slice(SHARE, 2 * SHARE), slice(kind * HW + at0.start, kind * HW + at0.stop)),
                )
        else:

            def adam_body(n, carry):
                cols = pl.ds(pl.multiple_of(n * SHARE, SHARE), SHARE)
                there = pl.ds(pl.multiple_of(at0.start + n * SHARE, SHARE), SHARE)
                if matrix == "u":
                    adam_block(cols, (slice(None), there), r.big, (slice(0, SHARE), there))
                else:
                    at = (there, slice(None))
                    adam_block(cols, at, getattr(r, "s" + matrix), at)
                return carry

            lax.fori_loop(0, width // SHARE, adam_body, 0)
        fresh = piece(fresh, name)
        if name in Y_FIRST:
            ay_copy(name, z, fresh).start()
        for direction in range(2):
            place, following = line(direction)

            @pl.when(place < NZ - 1)
            def _():
                az_copy(name, 0, direction, 0, 2 * z + y, fresh, following).start()

        if name not in Y_FIRST:
            ay_copy(name, z, fresh).start()
        local_out.append(local_copy(fresh, a_src(name, 2 * z + y), r.o_sem.at[p, 0]))
        local_out.append(
            local_copy(piece(grad_out, name), piece(getattr(r, matrix + "_grad"), name), r.o_sem.at[p, 1])
        )
        for k, (far, near) in enumerate(state_copies(name, True)):
            local_out.append(local_copy(near, far, state_sem(name, k)))

    def neighbour_share(name):
        part = a_src(name, 2 * z + 1 - y)
        ay_copy(name, z, part).wait_recv()
        for direction in range(2):
            place, following = line(direction)

            @pl.when(place < NZ - 1)
            def _():
                az_copy(name, 1, direction, 0, 2 * z + 1 - y, part, following).start()

    def gather_step(name, step):
        for side in range(2 if name in Y_FIRST else 1):
            for direction in range(2):
                place, following = line(direction)

                @pl.when(place >= step)
                def _():
                    source = z - step + 2 * step * direction
                    share = 2 * source + (1 - y if side else y)
                    part = a_src(name, share)
                    az_copy(name, side, direction, step - 1, share, part, following).wait_recv()
                    if step < NZ - 1:

                        @pl.when(place < NZ - 1)
                        def _():
                            az_copy(name, side, direction, step, share, part, following).start()

                    if name not in Y_FIRST:
                        ay_copy(name, source, part).start()

    def gather_end(name):
        part = a_src(name, 2 * z + y)

        def one(direction, carry):
            place, following = line(direction)

            @pl.when(place <= NZ - 2)
            def _():
                z_copy(name, direction, NZ - 2, following).wait_send()

            for step in range(NZ - 1):

                @pl.when((place >= step) & (place < NZ - 1))
                def _():
                    for side in range(2 if name in Y_FIRST else 1):
                        az_copy(name, side, direction, step, 2 * z + y, part, following).wait_send()

            return carry

        lax.fori_loop(0, 2, one, 0)
        if name in Z_FIRST:
            y_copy(name, 0).wait_send()
        if name in Y_FIRST:
            ay_copy(name, z, part).wait_send()

        def y_body(i, carry):
            if name not in Z_FIRST:
                y_copy(name, i).wait_send()
            if name not in Y_FIRST:
                there = a_src(name, 2 * i + y)
                ay_copy(name, i, there).wait_send()
                ay_copy(name, i, there).wait_recv()
            return carry

        lax.fori_loop(0, NZ, y_body, 0)

    def put_out(src, dst):
        cp = pltpu.make_async_copy(src, dst, r.stage_sem)
        cp.start()
        cp.wait()

    late = {}

    def turn(point):
        if not fast:
            return
        for kind, number in ORDER.get(point, ()):
            name = names_of[number] if number is not None else None
            if kind == V:
                late["vector_next"]()
            elif kind == Y:
                y_start(name)
            elif kind == F:
                finish_share(name)
            elif kind == E:
                y_exchange(name)
            elif kind == H:
                neighbour_share(name)
            elif kind in (C0, C1, C2):
                chain_step(name, kind - C0)
            else:
                gather_step(name, kind - G1 + 1)

    ag = {}
    for j in range(C):
        ag[j] = ag_send(0, j, r.g1)
    count_send(0)

    def w_copy(kind, src, block, device):
        return pltpu.make_async_remote_copy(
            src_ref=src, dst_ref=r.act.at[block], send_sem=r.ow_ss.at[kind],
            recv_sem=r.ow_rs.at[kind], device_id=device, device_id_type=MESH,
        )

    weights[0].wait()
    w_x = w_copy(0, r.wout, m, to_x)
    w_x.start()
    w_c = w_copy(1, r.wout, m, to_core)
    w_c.start()
    r.act[m] = r.wout[...]
    for w in qkv_weights:
        w.wait()

    def project(o):
        p = mm(r.g1[o], r.wqkv[...], NN)
        at = pl.ds(pl.multiple_of(o * R, R), R)
        for pair in range(PAIRS):
            rows = slice(pair * PAIR, (pair + 1) * PAIR)
            lanes = pl.ds(pl.multiple_of(m * HW + pair * PAIR, PAIR), PAIR)
            q, k, v = (p[:, qkv_lanes(pair, kind)] for kind in range(3))
            q = (q + r.vec[6:7, lanes]).astype(BF16)
            k = k.astype(BF16)
            v = (v + r.vec[7:8, lanes]).astype(BF16)
            for kind, value in enumerate((q, k, v)):
                r.qkv[at, qkv_lanes(pair, kind)] = value
            r.qT[rows, at] = q.T
            r.kT[rows, at] = k.T
            r.vT[rows, at] = v.T

    def make_dist(i, start):
        def one(b, carry):
            key = lax.broadcasted_iota(jnp.int32, (BQ, BQ), 0) + b * BQ
            query = lax.broadcasted_iota(jnp.int32, (BQ, BQ), 1) + i * BQ
            apart = query - key
            key_seg = r.segr[:, pl.ds(pl.multiple_of(b * BQ, BQ), BQ)]
            key_seg = jnp.broadcast_to(key_seg, (BQ, BQ)).T
            same = key_seg == r.segr[:, i * BQ : (i + 1) * BQ]
            r.big[b, :, start : start + BQ] = jnp.where((apart >= 0) & same, apart.astype(F32), jnp.inf)
            return carry

        lax.fori_loop(0, i + 1, one, 0)

    n_blocks = T // BQ
    project(m)
    for i in range(n_blocks):
        make_dist(i, i * BQ)
    count_next()
    for j in range(C):
        ag[j][1].wait()
    project(mc)
    for _ in range(1, dp_size.bit_length() - 1):
        count_next()
    fw = {}
    for j in range(C):
        ag[j][0].wait()
        fw[j] = ag_forward(0, j, r.g1)
    project(mx)
    for j in range(C):
        fw[j].wait()
    project(md)

    pair_row = lax.broadcasted_iota(jnp.int32, (2 * HD, BQ), 0) // HD
    pair_lane = lax.broadcasted_iota(jnp.int32, (BQ, 2 * HD), 1) // HD
    scale2 = log2_e / math.sqrt(HD)
    K_AT, V_AT, Q_AT, DIST = 0, HW, 2 * HW, 3 * HW

    def head_slope(h):
        head = jnp.zeros((1, BQ), jnp.int32) + (m * LOCAL_HEADS + h + 1)
        return jnp.exp2(head.astype(F32) * (-8.0 / HEADS)) * log2_e

    def pair_lanes(h, start):
        return pl.ds(pl.multiple_of(start + (h // 2) * PAIR, PAIR), PAIR)

    def kind_lanes(h, kind):
        return pl.ds(pl.multiple_of((h // 2) * 3 * PAIR + kind * PAIR, PAIR), PAIR)

    def head_scores(i, ke, h, start):
        mask = (pair_row == lax.rem(h, 2)).astype(F32).astype(BF16)
        q_cols = r.qT[pair_lanes(h, 0), i * BQ : (i + 1) * BQ] * mask
        raw = mm(r.qkv[0:ke, kind_lanes(h, 1)], q_cols, NN)
        return raw * scale2 - head_slope(h) * r.big[0 : i + 1, :, start : start + BQ].reshape(ke, BQ)

    OWN, PASSING = slice(0, HW), slice(HW, 2 * HW)

    def mix_copy(kind, j, src, dst, device):
        return pltpu.make_async_remote_copy(
            src_ref=src, dst_ref=dst, send_sem=r.mix_ss.at[kind, j], recv_sem=r.mix_rs.at[kind, j],
            device_id=device, device_id_type=MESH,
        )

    def send_mixture(i):
        for j in range(C):
            rows = slice(j * rc, (j + 1) * rc)
            src = r.mix.at[i * BQ + rows.start : i * BQ + rows.stop, :]

            @pl.when(i // 2 != chip)
            def _():
                kind = (core + i) % 2
                lanes = pl.ds(pl.multiple_of(kind * HW, HW), HW)
                mix_copy(kind, j, src, r.gup.at[m, rows, lanes], to_x).start()

            @pl.when(mc == i)
            def _():
                mix_copy(2, j, src, r.gup.at[m, rows, OWN], to_core).start()

            @pl.when(m == i)
            def _():
                r.gup[m, rows, OWN] = src[...]

    for turn_of, i in enumerate([*range(n_blocks - 2), n_blocks - 1, n_blocks - 2]):
        ke = (i + 1) * BQ
        block = slice(i * BQ, (i + 1) * BQ)

        def head_body(h, carry):
            s = head_scores(i, ke, h, i * BQ)
            top = jnp.max(s, 0, keepdims=True)
            e = jnp.exp2(s - top)
            total = jnp.sum(e, 0, keepdims=True)
            p = (e * (1.0 / total)).astype(BF16)
            r.lse[h, :, block] = top + jnp.log2(total)
            at = pl.ds(pl.multiple_of(h * HD, HD), HD)
            r.mixT[at, :] = mm(r.vT[at, 0:ke], p, NN).astype(BF16)
            return carry

        lax.fori_loop(0, LOCAL_HEADS, head_body, 0)
        r.mix[block, :] = r.mixT[...].T
        send_mixture(i)
        if turn_of >= n_blocks - (mp_size.bit_length() - 1):
            count_next()

    def pair_rows(ref, j):
        def of(first):
            v = ref[pl.ds(first, 2), pl.ds(j * rc, rc), :]
            return v.reshape(2 * rc, v.shape[2])

        return of

    def pair_flat(ref, j):
        def of(first):
            a = ref[pl.ds(pl.multiple_of(first * R + j * rc, rc), rc), :]
            b = ref[pl.ds(pl.multiple_of(first * R + R + j * rc, rc), rc), :]
            return jnp.concatenate([a, b], 0)

        return of

    def ag_finish(site, j, ref):
        ag[j][0].wait()
        cf = ag_forward(site, j, ref)
        ag[j][1].wait()
        cf.wait()

    w_x.wait()
    w_f = w_copy(2, r.act.at[mx], mx, to_core)
    w_f.start()
    m_f = {}
    for j in range(C):
        rows = slice(j * rc, (j + 1) * rc)
        here = r.gup.at[m, rows, OWN]
        mix_copy(1, j, here, here, to_x).wait_recv()
        m_f[j] = mix_copy(3, j, r.gup.at[mx, rows, PASSING], r.gup.at[mx, rows, OWN], to_core)
        m_f[j].start()
    w_c.wait()
    w_f.wait()
    rs = {}
    for j in range(C):
        rows = slice(j * rc, (j + 1) * rc)
        here = r.gup.at[m, rows, OWN]
        mix_copy(0, j, here, here, to_x).wait()
        mix_copy(1, j, here, here, to_x).wait_send()
        mix_copy(2, j, here, here, to_core).wait()
        m_f[j].wait()

        def out_body(n, carry):
            lanes = pl.ds(pl.multiple_of(n * TILE, TILE), TILE)
            total = mm(r.gup[0, rows, OWN], r.act[0, :, lanes], NN)
            for q in range(1, mp_size):
                total += mm(r.gup[q, rows, OWN], r.act[q, :, lanes], NN)
            r.keep[j, :, lanes] = total
            return carry

        lax.fori_loop(0, D // TILE, out_body, 0)
        hid = r.x[rows, :].astype(F32) + r.keep[j] + r.vec[2:3, :]
        r.hidden[rows, :] = hid
        normed, inverse = norm_rows(hid)
        r.n2[rows, :] = normed
        r.inv2[rows, :] = inverse
        ag[j] = ag_start(1, j, r.g2, (normed * r.vec[3:4, :] + r.vec[4:5, :]).astype(BF16))

    weights[1].wait()
    weights[2].wait()
    def up_half(j, first):
        pair = pl.ds(first, 2)
        rows = pair_rows(r.g2, j)(first)

        def up_body(n, carry):
            lanes = pl.ds(pl.multiple_of(n * TILE, TILE), TILE)
            u = mm(rows, r.wup[:, lanes], NN) + r.vec[pl.ds(8 + m, 1), lanes]
            a, b = gelu_both(u)
            r.act[pair, pl.ds(j * rc, rc), lanes] = a.astype(BF16).reshape(2, rc, TILE)
            r.big[pair, pl.ds(j * rc, rc), lanes] = b.reshape(2, rc, TILE)
            return carry

        lax.fori_loop(0, FU // TILE, up_body, 0)

    def by_halves(site, gather, ref, half, left, rhs_of):
        own = {}
        for j in range(C):
            ag[j][1].wait()
            half(j, 2 * chip)
            own[j] = rs_own(site, j, pair_rows(left, j), rhs_of)
        for j in range(C):
            ag[j][0].wait()
            ag_forward(gather, j, ref).wait()
            if site == 2 and j == C - 1:
                turn(THIRD)
            half(j, 2 * (1 - chip))
            cx, _ = rs_other(site, j, pair_rows(left, j), rhs_of)
            rs[j] = (cx, own[j])

    by_halves(1, 1, r.g2, up_half, r.act, lambda lanes: (r.wdown[:, lanes], NN))

    t_in.wait()
    loss_scale = token_total / r.cnt[len(bits), 0:1, 0:1]
    for j in range(C):
        rows = slice(j * rc, (j + 1) * rc)
        out = r.hidden[rows, :] + rs_finish(j, rs[j]) + r.vec[5:6, :]
        r.bo[rows, :] = out.astype(BF16)
        valid = jnp.broadcast_to(r.valid[:, rows].astype(F32), (SHARE, rc)).T[:, 0:1]
        grad = valid * (out - r.t[rows, :].astype(F32)) * loss_scale
        r.ig[rows, :] = grad
        ag[j] = ag_start(2, j, r.g3, grad.astype(BF16))
        r.vg[5:6, :] += jnp.sum(grad, 0, keepdims=True)
    bo_out = local_copy(r.bo, r.bo_hbm, r.in_sem.at[3])

    def act_half(j, first):
        pair = pl.ds(first, 2)
        rows = pair_rows(r.g3, j)(first)

        def act_body(n, carry):
            lanes = pl.ds(pl.multiple_of(n * TILE, TILE), TILE)
            ga = mm(rows, r.wdown[lanes, :], NT)
            gu = ga * r.big[pair, pl.ds(j * rc, rc), lanes].reshape(2 * rc, TILE)
            r.gup[pair, pl.ds(j * rc, rc), lanes] = gu.astype(BF16).reshape(2, rc, TILE)
            return carry

        lax.fori_loop(0, FU // TILE, act_body, 0)

    by_halves(2, 2, r.g3, act_half, r.gup, lambda lanes: (r.wup[lanes, :], NT))

    def whole_grad(left, right, width, dst):
        def body(n, carry):
            lanes = pl.ds(pl.multiple_of(n * TILE, TILE), TILE)
            r.stage[:, 0:width] = mm(right_tile(left, lanes), right[...].reshape(T, width), TN)
            put_out(r.stage.at[:, 0:width], dst.at[lanes, :])
            return carry

        lax.fori_loop(0, dst.shape[0] // TILE, body, 0)

    if not fast:
        whole_grad(r.act, r.g3, D, r.d_grad)

    for j in range(C):
        rows = slice(j * rc, (j + 1) * rc)
        gs = rs_finish(j, rs[j])
        gh = r.ig[rows, :] + norm_backward(gs, r.n2[rows, :], r.inv2[rows, :], r.vec[3:4, :])
        r.hidden[rows, :] = gh
        ag[j] = ag_start(3, j, r.g4, gh.astype(BF16))
        r.vg[2:3, :] += jnp.sum(gh, 0, keepdims=True)
        r.vg[3:4, :] += jnp.sum(gs * r.n2[rows, :], 0, keepdims=True)
        r.vg[4:5, :] += jnp.sum(gs, 0, keepdims=True)

    turn(NORM)
    if not fast:
        whole_grad(r.g2, r.gup, FU, r.u_grad)
    r.vg[pl.ds(8 + m, 1), :] = jnp.sum(r.gup[...].reshape(T, FU).astype(F32), 0, keepdims=True)

    for j in range(C):
        ag_finish(3, j, r.g4)

    def gm_body(o, carry):
        at = pl.ds(pl.multiple_of(o * R, R), R)
        gmx = mm(r.g4[o], r.wout[...], NT).astype(BF16)
        r.gm[at, :] = gmx
        r.vT[:, at] = gmx.T
        return carry

    lax.fori_loop(0, mp_size, gm_body, 0)
    turn(FOURTH)

    r.big[:, :, K_AT : K_AT + HW] = jnp.zeros((mp_size, R, HW), F32)
    r.big[:, :, V_AT : V_AT + HW] = jnp.zeros((mp_size, R, HW), F32)
    for pair in range(PAIRS):
        for i in range(n_blocks):
            ke = (i + 1) * BQ
            block = slice(i * BQ, (i + 1) * BQ)
            make_dist(i, DIST)

            def back_body(half, carry):
                h = 2 * pair + half
                row_mask = (pair_row == half).astype(F32).astype(BF16)
                lane_mask = (pair_lane == half).astype(F32).astype(BF16)
                lanes = slice(pair * PAIR, (pair + 1) * PAIR)
                p = jnp.exp2(head_scores(i, ke, h, DIST) - r.lse[h, :, block])
                gp = mm(r.qkv[0:ke, qkv_lanes(pair, 2)], r.vT[lanes, block] * row_mask, NN)
                inner = jnp.sum(p * gp, 0, keepdims=True)
                raw = (p * (gp - inner)).astype(BF16)
                low = p.astype(BF16)
                r.big[0 : i + 1, :, V_AT + lanes.start : V_AT + lanes.stop] += mm(
                    low, r.gm[block, lanes] * lane_mask, NN
                ).reshape(i + 1, BQ, PAIR)
                r.big[0 : i + 1, :, K_AT + lanes.start : K_AT + lanes.stop] += mm(
                    raw, r.qkv[block, qkv_lanes(pair, 0)] * lane_mask, NN
                ).reshape(i + 1, BQ, PAIR)
                at = pl.ds(pl.multiple_of(h * HD, HD), HD)
                r.big[i, at, Q_AT : Q_AT + BQ] = mm(r.kT[at, 0:ke], raw, NN) * (1.0 / math.sqrt(HD))
                return carry

            lax.fori_loop(0, 2, back_body, 0)
            rows = slice(pair * PAIR, (pair + 1) * PAIR)
            r.st[block, qkv_lanes(pair, 0)] = r.big[i, rows, Q_AT : Q_AT + BQ].T.astype(BF16)
            turn((pair, i))
        lanes = slice(pair * PAIR, (pair + 1) * PAIR)
        r.st[:, qkv_lanes(pair, 1)] = (
            r.big[:, :, K_AT + lanes.start : K_AT + lanes.stop].reshape(T, PAIR) * (1.0 / math.sqrt(HD))
        ).astype(BF16)
        r.st[:, qkv_lanes(pair, 2)] = (
            r.big[:, :, V_AT + lanes.start : V_AT + lanes.stop].reshape(T, PAIR).astype(BF16)
        )
        turn((pair,))
    for pair in range(PAIRS):
        lanes = pl.ds(pl.multiple_of(m * HW + pair * PAIR, PAIR), PAIR)
        for row, kind in ((6, 0), (7, 2)):
            r.vg[row : row + 1, lanes] = jnp.sum(
                r.st[:, qkv_lanes(pair, kind)].astype(F32), 0, keepdims=True
            )

    if fast:
        fetch_state("u")
        fetch_state("q")

    for j in range(C):
        rs[j] = rs_start(3, j, pair_flat(r.st, j), lambda lanes: (r.wqkv[lanes, :], NT))

    turn(BACK)
    if not fast:
        whole_grad(r.mix, r.g4, D, r.o_grad)
        whole_grad(r.g1, r.st, 3 * HW, r.q_grad)

    for j in range(C):
        rows = slice(j * rc, (j + 1) * rc)
        gf = rs_finish(j, rs[j])
        normed, inverse = norm_rows(r.x[rows, :].astype(F32))
        r.ig[rows, :] = r.hidden[rows, :] + norm_backward(gf, normed, inverse, r.vec[0:1, :])
        r.vg[0:1, :] += jnp.sum(gf * normed, 0, keepdims=True)
        r.vg[1:2, :] += jnp.sum(gf, 0, keepdims=True)
    ig_out = local_copy(r.ig, r.ig_hbm, r.in_sem.at[4])

    vector_send, vector_step = doubling(mp_bits + dp_bits, r.vs, r.vs_r, r.cnt_ss, r.cnt_rs)
    r.vs[0] = r.vg[...]
    vector_send(0)
    vector_out = []

    def vector_next():
        vector_step()
        late["steps"] = late.get("steps", 0) + 1
        if late["steps"] < len(bits):
            return
        vec_in.wait()
        total = r.vs[len(bits), 0 : r.vec.shape[0]]
        new = adam_step(total, r.vec_state[0], r.vec_state[1], r.vec_state[2], 0.0, token_total)
        r.v_sum[...] = total
        for k in range(3):
            r.vec_state[k] = new[k]
        r.v_copy[...] = new[0].astype(BF16)
        for k, (near, far) in enumerate(
            [(r.v_sum, r.v_grad), (r.vec_state, r.v_new), (r.v_copy, r.v_low)]
        ):
            vector_out.append(local_copy(near, far, r.in_sem.at[5 + k]))

    late["vector_next"] = vector_next
    if fast:
        turn(END)
        for name in parts:
            gather_end(name)
        for cp in local_out:
            cp.wait()
    else:
        for _ in bits:
            vector_next()
    for cp in [bo_out, ig_out] + vector_out:
        cp.wait()


Z_FIRST = ("d0",)
Y_FIRST = ("u1",)
Y, C0, C1, C2, E, F, H, G1, G2, G3, V = range(11)
D0, D1, U0, U1, O0, Q0, Q1 = range(7)
THIRD, NORM, FOURTH, BACK, END = range(5)
ORDER = {
    THIRD: ((Y, D1), (C0, D0),),
    NORM: ((C0, D1), (Y, U0), (C1, D0), (Y, U1), (C1, D1), (C2, D0),),
    FOURTH: ((C0, U0),),
    (0, 1): ((C2, D1),),
    (0, 2): ((E, D0),),
    (0,): ((Y, Q0),),
    (1, 0): ((C0, U1),),
    (1, 1): ((C1, U0),),
    (1, 2): ((C1, U1), (F, D1), (Y, O0),),
    (1, 3): ((F, D0), (C0, Q0), (C2, U1),),
    BACK: (
        (G1, D0), (Y, Q1), (C1, Q0), (G1, D1), (C2, U0), (C0, O0), (F, U1), (C2, Q0), (G2, D1),
    ),
    END: (
        (F, U0), (C1, O0), (C0, Q1), (G3, D1), (G2, D0), (F, Q0), (C2, O0), (V, None), (C1, Q1), (G1, U0),
        (H, U1), (V, None), (G1, Q0), (F, O0), (C2, Q1), (G2, U0), (G1, O0), (F, Q1), (G2, O0), (G2, Q0),
        (G3, Q0), (V, None), (G1, Q1), (G2, Q1), (G1, U1), (G3, U0), (V, None), (G3, Q1), (G2, U1), (G3, D0),
        (V, None), (G3, O0), (G3, U1),
    ),
}


def pieces(head_width, units):
    return [
        ("d0", units // 2),
        ("d1", units // 2),
        ("u0", units // 2),
        ("u1", units // 2),
        ("o0", head_width),
    ] + [("q%d" % pair, 6 * HD) for pair in range(head_width // (2 * HD))]


SHARE = 128


def block_call(sizes, x, teacher, segments, valid, vectors, copies, states):
    dp_size, mp_size = sizes
    R, D = x.shape
    T = mp_size * R
    wqkv, wout, wup, wdown = copies
    HW = wout.shape[0]
    FU = wup.shape[1]
    C = CHUNKS
    rc = R // C
    n_bits = (dp_size * mp_size).bit_length() - 1
    NZ = dp_size // 2
    PAIRS = HW // (2 * HD)
    fast = D == dp_size * SHARE
    dma = pltpu.SemaphoreType.DMA
    M = pltpu.VMEM
    S = jax.ShapeDtypeStruct
    vmem = pl.BlockSpec(memory_space=pltpu.VMEM)
    anywhere = pl.BlockSpec(memory_space=pl.ANY)

    ins = {
        "x_hbm": (x, anywhere),
        "t_hbm": (teacher, anywhere),
        "segr": (segments, vmem),
        "valid": (valid.reshape(1, R), vmem),
        "vec_low": (vectors, vmem),
        "vec_state_hbm": (states[4], anywhere),
        "wqkv_hbm": (wqkv, anywhere),
        "wout_hbm": (wout, anywhere),
        "wup_hbm": (wup, anywhere),
        "wdown_hbm": (wdown, anywhere),
    }
    outs = {
        "bo_hbm": (S((R, D), BF16), anywhere),
        "ig_hbm": (S((R, D), F32), anywhere),
        "v_grad": (S(vectors.shape, F32), anywhere),
        "v_new": (S(states[4].shape, F32), anywhere),
        "v_low": (S(vectors.shape, BF16), anywhere),
    }
    if fast:
        shard = {"q": (3, SHARE, HW), "o": (HW, SHARE), "u": (SHARE, FU), "d": (FU, SHARE)}
        whole = {"q": (3, D, HW), "o": (HW, D), "u": (D, FU), "d": (FU, D)}
        for name, state in zip("qoud", states):
            ins["s%s_hbm" % name] = (state, anywhere)
        for name in "qoud":
            outs[name + "_grad"] = (S(shard[name], F32), anywhere)
        for name in "qoud":
            outs[name + "_new"] = (S((3,) + shard[name], F32), anywhere)
        for name in "qoud":
            outs[name + "_full"] = (S(whole[name], BF16), anywhere)
    else:
        outs["q_grad"] = (S((D, 3 * HW), F32), anywhere)
        outs["o_grad"] = (S((HW, D), F32), anywhere)
        outs["u_grad"] = (S((D, FU), F32), anywhere)
        outs["d_grad"] = (S((FU, D), F32), anywhere)
    scratch = {
        "wqkv": M((D, 3 * HW), BF16),
        "wout": M((HW, D), BF16),
        "wup": M((D, FU), BF16),
        "wdown": M((FU, D), BF16),
        "w_sem": dma((3,)),
        "ow_ss": dma((3,)),
        "ow_rs": dma((3,)),
        "mix_ss": dma((4, C)),
        "mix_rs": dma((4, C)),
        "in_sem": dma((8,)),
        "x": M((R, D), BF16),
        "t": M((R, D), BF16),
        "bo": M((R, D), BF16),
        "ig": M((R, D), F32),
        "vec_state": M(states[4].shape, F32),
        "v_sum": M(vectors.shape, F32),
        "v_copy": M(vectors.shape, BF16),
        "wq_sem": dma((PAIRS, 3)),
        "vec": M(vectors.shape, F32),
        "g1": M((mp_size, R, D), BF16),
        "g2": M((mp_size, R, D), BF16),
        "g3": M((mp_size, R, D), BF16),
        "g4": M((mp_size, R, D), BF16),
        "qkv": M((T, 3 * HW), BF16),
        "qT": M((HW, T), BF16),
        "kT": M((HW, T), BF16),
        "vT": M((HW, T), BF16),
        "mixT": M((HW, BQ), BF16),
        "mix": M((T, HW), BF16),
        "lse": M((HW // HD, 1, T), F32),
        "hidden": M((R, D), F32),
        "n2": M((R, D), F32),
        "inv2": M((R, 1), F32),
        "act": M((mp_size, R, FU), BF16),
        "big": M((mp_size, R, FU), F32),
        "gup": M((mp_size, R, FU), BF16),
        "gm": M((T, HW), BF16),
        "st": M((T, 3 * HW), BF16),
        "pass_on": M((C, rc, D), F32),
        "keep": M((C, rc, D), F32),
        "rs_cs": M((C, 2, rc, D), BF16),
        "rs_cr": M((C, 2, rc, D), BF16),
        "rs_xs": M((C, rc, D), BF16),
        "rs_xr": M((C, rc, D), BF16),
        "cnt": M((n_bits + 1, 8, 128), F32),
        "cnt_r": M((n_bits, 8, 128), F32),
        "vg": M((16, D), F32),
        "vs": M((n_bits + 1, 16, D), F32),
        "vs_r": M((n_bits, 16, D), F32),
        "ag_ss": dma((4, C, 3)),
        "ag_rs": dma((4, C, 3)),
        "rs_ss": dma((3, C, 3)),
        "rs_rs": dma((3, C, 3)),
        "cnt_ss": dma((n_bits,)),
        "cnt_rs": dma((n_bits,)),
    }
    if fast:
        for name, w in pieces(HW, FU):
            shares = 1 if name in Z_FIRST else NZ
            rows = 2 * SHARE if name in Z_FIRST else SHARE
            scratch["ys" + name] = M((shares, SHARE, w), BF16)
            scratch["yr" + name] = M((shares, SHARE, w), BF16)
            scratch["zs" + name] = M((2, rows, w), BF16)
            scratch["zr" + name] = M((2, NZ - 1, rows, w), BF16)
        for name in "qoud":
            scratch["gr" + name] = M(shard[name], F32)
            scratch["nc" + name] = M(shard[name], BF16)
        scratch["sd"] = M((3,) + shard["d"], F32)
        scratch["so"] = M((3,) + shard["o"], F32)
        scratch["acc"] = M((SHARE, FU // 2), F32)
        scratch["wide"] = M((2 * SHARE, FU // 2), F32)
        n = len(pieces(HW, FU))
        scratch["s_sem"] = dma((n + 2 * PAIRS,))
        scratch["o_sem"] = dma((n, 2))
        scratch["y_ss"] = dma((n, NZ))
        scratch["y_rs"] = dma((n, NZ))
        scratch["z_ss"] = dma((n, 2))
        scratch["z_rs"] = dma((n, 2, NZ - 1))
        scratch["az_ss"] = dma((n + len(Y_FIRST), 2, NZ - 1))
        scratch["az_rs"] = dma((n + len(Y_FIRST), 2, NZ - 1))
        scratch["ay_ss"] = dma((n, NZ))
        scratch["ay_rs"] = dma((n, NZ))
    else:
        scratch["stage"] = M((TILE, D), F32)
        scratch["stage_sem"] = dma
    names = list(ins) + list(outs) + list(scratch)
    results = pl.pallas_call(
        functools.partial(block_kernel, sizes, fast, names),
        out_shape=[v[0] for v in outs.values()],
        in_specs=[v[1] for v in ins.values()],
        out_specs=[v[1] for v in outs.values()],
        scratch_shapes=list(scratch.values()),
        compiler_params=pltpu.CompilerParams(
            collective_id=0, has_side_effects=True, vmem_limit_bytes=62 << 20
        ),
        name="block",
    )(*[v[0] for v in ins.values()])
    outs = dict(zip(outs, results))
    if fast:
        names, results = list(outs), list(outs.values())
        outs = dict(zip(names, settle(results)))
    return outs, fast


def settle_kernel(count, *refs):
    sources, results, held = refs[:count], refs[count : 2 * count], refs[2 * count : 3 * count]
    in_sem, out_sem = refs[3 * count :]
    loads = [pltpu.make_async_copy(sources[i], held[i], in_sem.at[i]) for i in range(count)]
    stores = [pltpu.make_async_copy(held[i], results[i], out_sem.at[i]) for i in range(count)]
    for cp in loads:
        cp.start()
    for load, store in zip(loads, stores):
        load.wait()
        store.start()
    for cp in stores:
        cp.wait()


def settle(arrays):
    anywhere = pl.BlockSpec(memory_space=pltpu.HBM)
    dma = pltpu.SemaphoreType.DMA((len(arrays),))
    return pl.pallas_call(
        functools.partial(settle_kernel, len(arrays)),
        out_shape=[jax.ShapeDtypeStruct(a.shape, a.dtype) for a in arrays],
        in_specs=[anywhere] * len(arrays),
        out_specs=[anywhere] * len(arrays),
        scratch_shapes=[pltpu.VMEM(a.shape, a.dtype) for a in arrays] + [dma, dma],
        compiler_params=pltpu.CompilerParams(vmem_limit_bytes=62 << 20),
        name="settle",
    )(*arrays)


def adam_update(gradient, stored, decay_factor, token_total):
    new = adam_step(gradient, stored[0], stored[1], stored[2], decay_factor, token_total)
    return (jnp.stack(new), new[0].astype(jnp.bfloat16))


def shards(
    inputs,
    teacher,
    segments,
    valid_mask,
    qkv_copy,
    out_copy,
    up_copy,
    down_copy,
    vector_copy,
    qkv_state,
    out_state,
    up_state,
    down_state,
    vector_state,
):
    sizes = (lax.axis_size("dp"), lax.axis_size("mp"))
    token_total = inputs.shape[0] * sizes[0] * sizes[1]
    width = inputs.shape[1]
    head_width = qkv_copy.shape[2]
    pairs = head_width // (2 * HD)
    outs, fast = block_call(
        sizes,
        inputs,
        teacher,
        segments,
        valid_mask,
        vector_copy,
        (qkv_copy.transpose(1, 0, 2), out_copy, up_copy, down_copy),
        (qkv_state.transpose(0, 2, 1, 3), out_state, up_state, down_state, vector_state),
    )
    vector_grad, vector_new, vector_low = outs["v_grad"], outs["v_new"], outs["v_low"]
    if fast:
        qkv_grad = outs["q_grad"].transpose(1, 0, 2)
        out_grad, up_grad, down_grad = (outs[n + "_grad"] for n in "oud")
        qkv_new = outs["q_new"].transpose(0, 2, 1, 3)
        out_new, up_new, down_new = (outs[n + "_new"] for n in "oud")
        qkv_full = outs["q_full"].transpose(1, 0, 2)
        out_full, up_full, down_full = (outs[n + "_full"] for n in "oud")
    else:
        qkv_local = outs["q_grad"].reshape(width, pairs, 3, 2 * HD)
        qkv_local = qkv_local.transpose(0, 2, 1, 3).reshape(width, 3, head_width)
        qkv_grad, out_grad, up_grad, down_grad = (
            lax.psum_scatter(qkv_local, "dp", scatter_dimension=0, tiled=True),
            lax.psum_scatter(outs["o_grad"], "dp", scatter_dimension=1, tiled=True),
            lax.psum_scatter(outs["u_grad"], "dp", scatter_dimension=0, tiled=True),
            lax.psum_scatter(outs["d_grad"], "dp", scatter_dimension=1, tiled=True),
        )
        qkv_new, qkv_low = adam_update(qkv_grad, qkv_state, decay_rate, token_total)
        out_new, out_low = adam_update(out_grad, out_state, decay_rate, token_total)
        up_new, up_low = adam_update(up_grad, up_state, decay_rate, token_total)
        down_new, down_low = adam_update(down_grad, down_state, decay_rate, token_total)
        qkv_full, out_full, up_full, down_full = (
            lax.all_gather(qkv_low, "dp", axis=0, tiled=True),
            lax.all_gather(out_low, "dp", axis=1, tiled=True),
            lax.all_gather(up_low, "dp", axis=0, tiled=True),
            lax.all_gather(down_low, "dp", axis=1, tiled=True),
        )
    return (
        outs["bo_hbm"],
        outs["ig_hbm"],
        qkv_grad,
        out_grad,
        up_grad,
        down_grad,
        vector_grad,
        qkv_new,
        out_new,
        up_new,
        down_new,
        vector_new,
        qkv_full,
        out_full,
        up_full,
        down_full,
        vector_low,
    )


def solution(mesh):
    in_specs = (
        P(("dp", "mp"), None),
        P(("dp", "mp"), None),
        P("dp", None),
        P(("dp", "mp")),
        P(None, None, "mp"),
        P("mp", None),
        P(None, "mp"),
        P("mp", None),
        P(),
        P(None, "dp", None, "mp"),
        P(None, "mp", "dp"),
        P(None, "dp", "mp"),
        P(None, "mp", "dp"),
        P(),
    )
    out_specs = (
        P(("dp", "mp"), None),
        P(("dp", "mp"), None),
        P("dp", None, "mp"),
        P("mp", "dp"),
        P("dp", "mp"),
        P("mp", "dp"),
        P(),
        P(None, "dp", None, "mp"),
        P(None, "mp", "dp"),
        P(None, "dp", "mp"),
        P(None, "mp", "dp"),
        P(),
        P(None, None, "mp"),
        P("mp", None),
        P(None, "mp"),
        P("mp", None),
        P(),
    )
    return jax.shard_map(shards, mesh=mesh, in_specs=in_specs, out_specs=out_specs, check_vma=False)
```

profile of v0, /device:TPU:0, one launch (start us, length us, event | category | flops | bytes accessed | tf_op | source)
XLA Modules:
  0.0 222.5 jit_solution(7094037726648505735)
XLA Ops:
  0.7 211.0 %block.1 = (bf16[256,1024]{1,0:T(8,128)(2,1)}, f32[256,1024]{1,0:T(8,128)}, f32[12,1024]{1,0:T(8,128)}, f32[3,12,1024]{2,1,0:T(8,128)}, bf16[12,1024]{1,0:T(8,12...) custom-call(bf16[256,1024]{1,0:T(8,128)(2,1)} %refs_0_.1, ...), custom_call_target="tpu_custom_call" | custom-call | tf_op jit(solution)/shard_map/block/pallas_call | solution.py:1225
  211.7 10.6 %settle.1 = (bf16[256,1024]{1,0:T(8,128)(2,1)}, f32[256,1024]{1,0:T(8,128)}, f32[12,1024]{1,0:T(8,128)}, f32[3,12,1024]{2,1,0:T(8,128)}, bf16[12,1024]{1,0:T(8,1...) custom-call(bf16[256,1024]{1,0:T(8,128)(2,1)} %get-tuple-element.51., ...), custom_call_target="tpu_custom_call" | custom-call | tf_op jit(solution)/shard_map/settle/pallas_call | solution.py:1260
where the time goes:
time: 223 us; the launch traced here: 222 us
  Pallas kernels  222 us (100%)
    pallas_call x1, Pallas kernels, block_call(): pl.pallas_call(functools.partial(block_kernel, sizes, fast, names), out_s...  211 us
    pallas_call x1, Pallas kernels, settle(): pl.pallas_call(functools.partial(settle_kernel, len(arrays)), out_shape=[...  10.6 us

commit v1 on v0

--- a/solution.py
+++ b/solution.py
@@ -771,7 +771,7 @@
             r.mixT[at, :] = mm(r.vT[at, 0:ke], p, NN).astype(BF16)
             return carry
 
-        lax.fori_loop(0, LOCAL_HEADS, head_body, 0)
+        lax.fori_loop(0, LOCAL_HEADS, head_body, 0, unroll=LOCAL_HEADS if i < n_blocks // 2 else 1)
         r.mix[block, :] = r.mixT[...].T
         send_mixture(i)
         if turn_of >= n_blocks - (mp_size.bit_length() - 1):

time: 223 us -> 223 us (level)
  no operation moved by 1% of the time
where the time goes in v1:
time: 223 us; the launch traced here: 222 us
  Pallas kernels  222 us (100%)
    pallas_call x1, Pallas kernels, block_call(): pl.pallas_call(functools.partial(block_kernel, sizes, fast, names), out_s...  211 us
    pallas_call x1, Pallas kernels, settle(): pl.pallas_call(functools.partial(settle_kernel, len(arrays)), out_shape=[...  10.6 us

profile of v1, /device:TPU:0, one launch (start us, length us, event | category | flops | bytes accessed | tf_op | source)
XLA Modules:
  0.0 222.4 jit_solution(2699674894302507318)
XLA Ops:
  0.7 211.0 %block.1 = (bf16[256,1024]{1,0:T(8,128)(2,1)}, f32[256,1024]{1,0:T(8,128)}, f32[12,1024]{1,0:T(8,128)}, f32[3,12,1024]{2,1,0:T(8,128)}, bf16[12,1024]{1,0:T(8,12...) custom-call(bf16[256,1024]{1,0:T(8,128)(2,1)} %refs_0_.1, ...), custom_call_target="tpu_custom_call" | custom-call | tf_op jit(solution)/shard_map/block/pallas_call | solution.py:1225
  211.6 10.6 %settle.1 = (bf16[256,1024]{1,0:T(8,128)(2,1)}, f32[256,1024]{1,0:T(8,128)}, f32[12,1024]{1,0:T(8,128)}, f32[3,12,1024]{2,1,0:T(8,128)}, bf16[12,1024]{1,0:T(8,1...) custom-call(bf16[256,1024]{1,0:T(8,128)(2,1)} %get-tuple-element.51., ...), custom_call_target="tpu_custom_call" | custom-call | tf_op jit(solution)/shard_map/settle/pallas_call | solution.py:1260
